TPU v7x, 1024 devices: a whole 8x8x8 slice. The times are simulated.
1024 devices in a mesh: group: 16 (over y, core), outer: 64 (over z, x).
Axes of the slice: x: 8, y: 8, z: 8, core: 2. Of those that a mesh axis runs over, the one named last changes fastest.
Arguments:
- features: bfloat16 [262144, 1024], P(('group', 'outer')), may hold values from -6 to 6
- basis_weights: bfloat16 [2, 1024, 512], replicated, may hold values from -0.1875 to 0.1875
- self_weight: bfloat16 [1024, 512], replicated, may hold values from -0.1875 to 0.1875
- coefficients: float32 [3, 2], replicated, may hold values from -4 to 4
- counts: int32 [2048, 3, 4, 128, 128], P(('group', 'outer')), may hold values from 0 to 3, as said below
- tile_source: int32 [2048, 3, 4], P(('group', 'outer')), may hold values from 0 to 5, as said below
- send_rows: int32 [16384, 16], P(('group', 'outer')), may hold values from 0 to 255
- edge_rows: int32 [2048, 128], P(('group', 'outer')), may hold values from 0 to 255
- cotangent: bfloat16 [262144, 512], P(('group', 'outer')), may hold values from -24 to 24
Outputs:
- layer_out: bfloat16 [262144, 512], P(('group', 'outer'))
- basis_grad: float32 [2, 1024, 512], P(None, 'group', 'outer')
Inputs may be any that keep to these rules, and one draw needn't show every extreme that they name: `counts`: for each destination block and relation the tiles that hold an edge come first: after the first all-zero tile every later tile of that block and relation is zero. The first tile always holds an edge, and some destination block and relation has all 4 tiles holding edges. `tile_source`: on each partition the first tiles of its 6 destination blocks and relations name all 6 source blocks.
All inputs are finite; a program needn't handle non-finite values.
Results may differ from a plain program's by a relative error of at most 0.0048.
Values may be sent and summed in bfloat16 or wider, within the bound.
A program may use at most 32 MiB of HBM per device.

v0:
```python
import math

import jax
import jax.numpy as jnp
from jax import lax
from jax.sharding import PartitionSpec as P


def with_halo(block, sides, width):
    for axis, dim in sides:
        count = lax.axis_size(axis)
        forward = [(i, i + 1) for i in range(count - 1)]
        forward.append((count - 1, 0))
        backward = [(target, source) for source, target in forward]
        low = lax.ppermute(
            lax.slice_in_dim(block, block.shape[dim] - width, None, axis=dim), axis, forward
        )
        high = lax.ppermute(lax.slice_in_dim(block, 0, width, axis=dim), axis, backward)
        block = jnp.concatenate([low, block, high], axis=dim)
    return block


def shards(
    features,
    basis_weights,
    self_weight,
    coefficients,
    counts,
    tile_source,
    send_rows,
    edge_rows,
    cotangent,
):
    row_count = features.shape[0]
    feature_width = features.shape[1]
    groups = lax.axis_size("group")
    outers = lax.axis_size("outer")
    peer_rows = send_rows.shape[1]
    rim_rows = edge_rows.shape[1]
    blocks = counts.shape[0]
    relations = counts.shape[1]
    tile_slots = counts.shape[2]
    block_rows = counts.shape[3]
    basis_count = basis_weights.shape[0]
    outgoing = jnp.take(features, send_rows.reshape(-1), axis=0).reshape(
        groups, peer_rows, feature_width
    )
    incoming = lax.all_to_all(outgoing, "group", split_axis=0, concat_axis=0, tiled=True).reshape(
        groups * peer_rows, feature_width
    )
    boundary_rows = jnp.take(features, edge_rows.reshape(-1), axis=0)
    padded = with_halo(boundary_rows, (("outer", 0),), rim_rows)
    sources = jnp.concatenate(
        [features, incoming, padded[:rim_rows], padded[padded.shape[0] - rim_rows :]], 0
    )
    source_count = sources.shape[0] // block_rows
    stacked = sources.reshape(source_count, block_rows, feature_width)
    chosen = jnp.take(stacked, tile_source.reshape(-1), axis=0).reshape(
        blocks, relations, tile_slots, block_rows, feature_width
    )
    aggregate = jnp.einsum(
        "drkij,drkjh->drih", counts.astype(jnp.bfloat16), chosen, preferred_element_type=jnp.float32
    )
    degree = jnp.sum(counts, axis=(2, 4))
    normalized = aggregate / jnp.maximum(degree, 1).astype(jnp.float32)[..., None]
    mixed_list = []
    for basis_index in range(basis_count):
        combined = coefficients[0, basis_index] * normalized[:, 0]
        for relation in range(1, relations):
            combined = combined + coefficients[relation, basis_index] * normalized[:, relation]
        mixed_list.append(combined.reshape(row_count, feature_width))
    mixed_rows = jnp.stack(mixed_list).astype(jnp.bfloat16)
    grad_term = jnp.einsum("bnh,no->bho", mixed_rows, cotangent, preferred_element_type=jnp.float32)
    reduced = lax.psum_scatter(grad_term, "outer", scatter_dimension=2, tiled=True)
    reduced = lax.psum_scatter(reduced, "group", scatter_dimension=1, tiled=True)
    grad_scale = 1.0 / math.sqrt(row_count * groups * outers)
    basis_grad = reduced * grad_scale
    layer_rows = jnp.dot(features, self_weight, preferred_element_type=jnp.float32)
    for basis_index in range(basis_count):
        layer_rows = layer_rows + jnp.dot(
            mixed_rows[basis_index], basis_weights[basis_index], preferred_element_type=jnp.float32
        )
    layer_out = layer_rows.astype(jnp.bfloat16)
    return (layer_out, basis_grad)


def solution(mesh):
    return jax.shard_map(
        shards,
        mesh=mesh,
        in_specs=(
            P(("group", "outer"), None),
            P(),
            P(),
            P(),
            P(("group", "outer"), None, None, None, None),
            P(("group", "outer"), None, None),
            P(("group", "outer"), None),
            P(("group", "outer"), None),
            P(("group", "outer"), None),
        ),
        out_specs=(P(("group", "outer"), None), P(None, "group", "outer")),
        check_vma=False,
    )
```

profile of v0, /device:TPU:113, one launch (start us, length us, event | category | flops | bytes accessed | tf_op | source)
XLA Modules:
  0.0 388.1 jit_solution(4313529218231172305)
XLA Ops:
  7.2 0.0 copy-start
  7.2 0.9 reshape.160
  8.1 0.0 copy-start.7
  8.1 0.0 copy-start.1
  8.1 2.7 gather_fusion.1
  10.8 0.9 broadcast_select_fusion.1
  11.8 15.4 %all-to-all-start = ((bf16[16,16,1024]{2,1,0:T(8,128)(2,1)}), bf16[16,16,1024]{2,1,0:T(8,128)(2,1)S(1)}, u32[]{:S(2)}, u32[]{:S(2)}) async-start(bf16[16,16,1024]{2,1,0:T(8,128)(2,1)} %bitcast.1), calls=%async_computation | async-start | bytes 1048576 | tf_op jit(solution)/shard_map/all_to_all | solution.py:48
  27.1 0.0 reduce-scatter.5.cloned.1.call-start
  27.2 0.0 copy-done.7
  27.2 0.0 copy-done.1
  27.2 0.0 copy-start.5
  27.3 0.0 copy-start.6
  27.3 1.2 gather_fusion.2
  28.4 0.1 broadcast_select_fusion
  28.6 1.9 collective-permute-start
  30.5 10.8 %collective-permute-start.1 = (bf16[128,1024]{1,0:T(8,128)(2,1)S(1)}, bf16[128,1024]{1,0:T(8,128)(2,1)S(1)}, u32[]{:S(2)}, u32[]{:S(2)}) collective-permute-start(bf16[128,1024]{1,0:T(8,128)(2,1)S(1)} %get-tuple-element.6), channel_id=1, source_target_pairs={{1,0},{2,1},{3,2},{4,3},{5,4},{6,5},{7,6},{8,7},{9,8},{10,9},{11,1... | collective-permute-start | bytes 786440 | tf_op jit(solution)/shard_map/ppermute | solution.py:18
  41.4 0.0 copy-done.5
  41.4 0.1 reshape.165
  41.5 0.0 copy-done.6
  41.5 0.7 fusion.22
  42.2 1.6 reduce_sum.9
  43.8 2.0 collective-permute-done
  45.8 0.9 collective-permute-done.1
  46.7 0.0 copy-start.3
  46.7 0.0 all-to-all-done
  46.7 0.7 copy-done.3
  47.4 0.8 copy-done.2
  48.2 1.2 pad_maximum_fusion
  49.4 4.4 %gather_fusion = bf16[24,128,1024]{2,1,0:T(8,128)(2,1)} fusion(bf16[6,128,1024]{2,1,0:T(8,128)(2,1)S(1)} %bitcast.43, s32[1024]{0:T(1024)S(1)} %pad_clamp_fusion), kind=kCustom, calls=%fused_computation.2 | custom fusion | bytes 12583008 | tf_op jit(solution)/shard_map/jit(_take)/gather | solution.py:58
  53.8 4.8 %fusion.3 = f32[2,3,128,1024]{3,2,1,0:T(8,128)S(1)} fusion(f32[2,3,128]{2,1,0:T(4,128)S(1)} %maximum_convert_fusion, bf16[2,3,4,128,1024]{4,3,2,1,0:T(8,128)(2,1)} %bitcast.44, pred[2,3,4]{2,1,0:T(4,128)(4,1)S(1)} %copy.17, s32[2,3,4,128,128]{4,3,2,1,0:T(8,128)} %param.15), kind=kOutput, calls=%fused_computation.7 | convolution fusion | flops 809631744 | bytes 11013144 | tf_op jit(solution)/shard_map/drkij,drkjh->drih/dot_general | solution.py:61
  58.6 0.0 copy-start.4
  58.6 4.2 %add_convert_fusion = (bf16[2,1,128,1024]{3,2,1,0:T(8,128)(2,1)S(1)}, bf16[2,1,128,1024]{3,2,1,0:T(8,128)(2,1)S(1)}) fusion(f32[2,3,128,1024]{3,2,1,0:T(8,128)S(1)} %fusion.3, f32[]{:T(128)} %bitcast.16, f32[]{:T(128)} %bitcast.15, f32[]{:T(128)} %bitcast.14, f32[]{:T(128)} %bitcast.11, f32[]{:T(128)} %bitcast.10, f32[]{:T(128)} %bitcast), kind=kLoop, calls=%fused_computation.20 | loop fusion | flops 3145728 | bytes 4194328 | tf_op jit(solution)/shard_map/convert.2
  62.8 0.0 copy-done.4
  62.8 2.7 fusion.6
  65.5 0.0 reduce-scatter.5.cloned.1.call-update
  65.6 0.0 reduce-scatter.7.cloned.1.call-start
  65.6 0.0 copy-done
  65.6 0.4 fusion.23
  66.1 1.7 convolution_add_fusion.1
  67.7 245.0 %reduce-scatter.5.cloned.1.call-done = f32[2,1024,8]{1,2,0:T(8,128)} async-done(((f32[2,1024,512]{1,2,0:T(8,128)}), f32[2,1024,8]{1,2,0:T(8,128)}) %reduce-scatter.5.cloned.1.call-update) | async-done | bytes 65552 | tf_op jit(solution)/shard_map/reduce_scatter | solution.py:74
  312.7 1.3 copy.23
  314.0 1.4 reshape.198
  315.4 0.0 reduce-scatter.7.cloned.1.call-update
  315.4 2.4 fusion.5
  317.8 62.0 %reduce-scatter.7.cloned.1.call-done = f32[64,16]{1,0:T(8,128)} async-done(((f32[1024,16]{1,0:T(8,128)}), f32[64,16]{1,0:T(8,128)}) %reduce-scatter.7.cloned.1.call-update) | async-done | bytes 4112
  379.8 0.9 reshape.199
  380.6 0.1 copy.24
  380.7 0.6 broadcast_multiply_fusion
  (14 shorter events, 0.1 us)
Async XLA Ops:
  7.2 58.5 %copy-start = (bf16[1024,512]{1,0:T(8,128)(2,1)S(1)}, bf16[1024,512]{1,0:T(8,128)(2,1)}, u32[]{:S(2)}) copy-start(bf16[1024,512]{1,0:T(8,128)(2,1)} %param.13) | copy-start | bytes 3145732
  8.1 19.1 %copy-start.7 = (s32[2,128]{1,0:T(2,128)S(1)}, s32[2,128]{1,0:T(2,128)}, u32[]{:S(2)}) copy-start(s32[2,128]{1,0:T(2,128)} %param.18) | copy-start | bytes 3076
  8.1 19.2 %copy-start.1 = (bf16[256,1024]{1,0:T(8,128)(2,1)S(1)}, bf16[256,1024]{1,0:T(8,128)(2,1)}, u32[]{:S(2)}) copy-start(bf16[256,1024]{1,0:T(8,128)(2,1)} %param.11) | copy-start | bytes 1572868
  11.8 34.9 %all-to-all-start = ((bf16[16,16,1024]{2,1,0:T(8,128)(2,1)}), bf16[16,16,1024]{2,1,0:T(8,128)(2,1)S(1)}, u32[]{:S(2)}, u32[]{:S(2)}) async-start(bf16[16,16,1024]{2,1,0:T(8,128)(2,1)} %bitcast.1), calls=%async_computation | async-start | bytes 1048576 | tf_op jit(solution)/shard_map/all_to_all | solution.py:48
  27.1 285.6 %reduce-scatter.5.cloned.1.call-start = ((), (), s32[]{:S(2)}) async-start(), calls=%async_computation.3 | async-start | bytes 4259840 | tf_op jit(solution)/shard_map/reduce_scatter | solution.py:74
  27.2 14.1 %copy-start.5 = (s32[2,3,4]{2,0,1:T(2,128)S(1)}, s32[2,3,4]{2,0,1:T(2,128)}, u32[]{:S(2)}) copy-start(s32[2,3,4]{2,0,1:T(2,128)} %param.16) | copy-start | bytes 292
  27.3 14.2 %copy-start.6 = (f32[3,2]{0,1:T(2,128)S(1)}, f32[3,2]{0,1:T(2,128)}, u32[]{:S(2)}) copy-start(f32[3,2]{0,1:T(2,128)} %param.14) | copy-start | bytes 76
  28.6 17.2 %collective-permute-start = (bf16[128,1024]{1,0:T(8,128)(2,1)S(1)}, bf16[128,1024]{1,0:T(8,128)(2,1)S(1)}, u32[]{:S(2)}, u32[]{:S(2)}) collective-permute-start(bf16[128,1024]{1,0:T(8,128)(2,1)S(1)} %get-tuple-element.5), channel_id=1, source_target_pairs={{0,1},{1,2},{2,3},{3,4},{4,5},{5,6},{6,7},{7,8},{8,9},{9,10},{10,1... | collective-permute-start | bytes 786440 | tf_op jit(solution)/shard_map/ppermute | solution.py:15
  30.5 16.1 %collective-permute-start.1 = (bf16[128,1024]{1,0:T(8,128)(2,1)S(1)}, bf16[128,1024]{1,0:T(8,128)(2,1)S(1)}, u32[]{:S(2)}, u32[]{:S(2)}) collective-permute-start(bf16[128,1024]{1,0:T(8,128)(2,1)S(1)} %get-tuple-element.6), channel_id=1, source_target_pairs={{1,0},{2,1},{3,2},{4,3},{5,4},{6,5},{7,6},{8,7},{9,8},{10,9},{11,1... | collective-permute-start | bytes 786440 | tf_op jit(solution)/shard_map/ppermute | solution.py:18
  46.7 0.7 copy-start.3
  47.4 0.8 copy-start.2
  58.6 4.3 %copy-start.4 = (bf16[256,512]{1,0:T(8,128)(2,1)S(1)}, bf16[256,512]{1,0:T(8,128)(2,1)}, u32[]{:S(2)}) copy-start(bf16[256,512]{1,0:T(8,128)(2,1)} %param.19) | copy-start | bytes 786436
  65.6 314.2 %reduce-scatter.7.cloned.1.call-start = ((), (), s32[]{:S(2)}) async-start(), calls=%async_computation.4 | async-start | bytes 557056
Sparse Core Ops, SparseCore 0:
  65.7 246.9 reduce-scatter.4
  316.4 63.2 reduce-scatter.6
where the time goes:
time: 390 us; the launch traced here: 388 us
  waiting for transfers between devices  310 us (79%)
  starting transfers between devices  28.2 us (7%)
  local copies, waits for them, and re-layouts  15 us (4%)
  between operations  14.3 us (4%)
  matrix products  11.9 us (3%)
  other arithmetic  8.79 us (2%)
    reduce_scatter x1, waiting for transfers between devices, shards(): lax.psum_scatter(grad_term, 'outer', scatter_dimension=2, tiled=True)  245 us
    unnamed x3, waiting for transfers between devices  62 us
    all_to_all x1, starting transfers between devices, shards(): lax.all_to_all(outgoing, 'group', split_axis=0, concat_axis=0, tiled=True)  15.4 us
    ppermute x1, starting transfers between devices, with_halo(): lax.ppermute(lax.slice_in_dim(block, 0, width, axis=dim), axis, backward)  10.8 us
  transfers between devices with their start and end apart: 5, of which 4 were waited for; matrix products, arithmetic and copies ran while one was open for 2% of the time, Pallas kernels for 0%

commit v1 on v0

v1 whole, which is shorter than its diff:
```python
import functools
import math

import jax
import jax.numpy as jnp
from jax import lax
from jax.experimental import pallas as pl
from jax.experimental.pallas import tpu as pltpu
from jax.sharding import PartitionSpec as P

MESH = pl.DeviceIdType.MESH
CHUNKS = 4
F32 = jnp.float32
BF16 = jnp.bfloat16


def dot(a, b):
    return jnp.dot(a, b, preferred_element_type=F32)


def one_hot_of(column, width):
    lanes = lax.broadcasted_iota(jnp.int32, (column.shape[0], width), 1)
    return (lanes == column).astype(F32).astype(BF16)


def layer_kernel(
    sizes,
    features,
    basis_hbm,
    self_hbm,
    coefficients,
    counts_hbm,
    tile_source,
    send_rows,
    edge_rows,
    cotangent_hbm,
    layer_hbm,
    grad_out,
    counts,
    basis,
    own_weight,
    cotangent,
    cot_t,
    adjacency,
    weight_of,
    outgoing,
    arrived,
    mixed,
    layer,
    core_out,
    core_in,
    total,
    first_out,
    first_in,
    second_out,
    second_in,
    third_out,
    third_in,
    turned,
    load_sem,
    a_send,
    a_recv,
    c_send,
    c_recv,
    f_send,
    f_recv,
    s_send,
    s_recv,
    t_send,
    t_recv,
):
    groups, zs, xs, chunks, relations, slots, block = sizes
    g = lax.axis_index("group")
    o = lax.axis_index("outer")
    z, x = o // xs, o % xs
    core = g % 2
    rows, width = features.shape
    out_cols = cotangent.shape[1]
    peer_rows = send_rows.shape[1]
    blocks = rows // block
    pairs = blocks * relations
    part = width // chunks
    half = part // 2
    incoming = groups * peer_rows
    sources = adjacency.shape[1] // block
    z_rows = out_cols // zs
    tail = z_rows // xs

    barrier = pltpu.get_barrier_semaphore()

    def greet(group, outer):
        pl.semaphore_signal(
            barrier, inc=1, device_id={"group": group, "outer": outer}, device_id_type=MESH
        )

    def greet_group(i, carry):
        greet((g + i) % groups, o)
        return carry

    def greet_x(i, carry):
        greet(g, z * xs + (x + i) % xs)
        return carry

    def greet_z(i, carry):
        greet(g, ((z + i) % zs) * xs + x)
        return carry

    upper = (o + 1) % (zs * xs)
    lower = (o + zs * xs - 1) % (zs * xs)
    lax.fori_loop(1, groups, greet_group, 0)
    lax.fori_loop(1, xs, greet_x, 0)
    lax.fori_loop(1, zs, greet_z, 0)
    greet(g, upper)
    greet(g, lower)

    loads = [
        pltpu.make_async_copy(counts_hbm, counts, load_sem.at[0]),
        pltpu.make_async_copy(cotangent_hbm, cotangent, load_sem.at[1]),
        pltpu.make_async_copy(self_hbm, own_weight, load_sem.at[2]),
        pltpu.make_async_copy(basis_hbm, basis, load_sem.at[3]),
    ]
    for load in loads:
        load.start()

    slot_rows = jnp.broadcast_to(
        send_rows[...][:, None, :], (groups, peer_rows, peer_rows)
    ).reshape(incoming, peer_rows)
    at = lax.broadcasted_iota(jnp.int32, (incoming, peer_rows), 0) % peer_rows
    lane = lax.broadcasted_iota(jnp.int32, (incoming, peer_rows), 1)
    peer_index = jnp.sum(jnp.where(at == lane, slot_rows, 0), axis=1, keepdims=True)
    rim = edge_rows.shape[1]
    at = lax.broadcasted_iota(jnp.int32, (rim, rim), 0)
    lane = lax.broadcasted_iota(jnp.int32, (rim, rim), 1)
    rim_index = [
        jnp.sum(
            jnp.where(at == lane, jnp.broadcast_to(edge_rows[side : side + 1, :], (rim, rim)), 0),
            axis=1,
            keepdims=True,
        )
        for side in (0, 1)
    ]
    pick = one_hot_of(jnp.concatenate([peer_index] + rim_index, axis=0), rows)
    for c in range(chunks):
        outgoing[c] = dot(pick, features[:, c * part : (c + 1) * part]).astype(BF16)

    pl.semaphore_wait(barrier, groups - 1 + xs - 1 + zs - 1 + 2)

    own = pl.ds(pl.multiple_of(g * peer_rows, peer_rows), peer_rows)
    for c in range(chunks):

        def send_peer(i, carry, c=c):
            q = (g + i) % groups
            theirs = pl.ds(pl.multiple_of(q * peer_rows, peer_rows), peer_rows)
            pltpu.make_async_remote_copy(
                src_ref=outgoing.at[c, theirs],
                dst_ref=arrived.at[c, own],
                send_sem=a_send.at[c],
                recv_sem=a_recv.at[c],
                device_id={"group": q, "outer": o},
                device_id_type=MESH,
            ).start()
            return carry

        lax.fori_loop(1, groups, send_peer, 0)
        pltpu.make_async_copy(outgoing.at[c, own], arrived.at[c, own], a_recv.at[c]).start()
        for neighbour, start, land in (
            (lower, incoming, incoming + rim),
            (upper, incoming + rim, incoming),
        ):
            pltpu.make_async_remote_copy(
                src_ref=outgoing.at[c, start : start + rim],
                dst_ref=arrived.at[c, land : land + rim],
                send_sem=a_send.at[c],
                recv_sem=a_recv.at[c],
                device_id={"group": g, "outer": neighbour},
                device_id_type=MESH,
            ).start()

    loads[0].wait()

    def build(p, carry):
        t, r = p // relations, p % relations
        tiles = [counts[t, r, k].astype(F32) for k in range(slots)]
        named = [tile_source[t, r, k] for k in range(slots)]
        at_rows = pl.ds(pl.multiple_of(p * block, block), block)
        for s in range(sources):
            held = jnp.zeros((block, block), F32)
            for k in range(slots):
                held = held + jnp.where(named[k] == s, tiles[k], 0.0)
            adjacency[at_rows, s * block : (s + 1) * block] = held.astype(BF16)
        degree = jnp.sum(sum(tiles[1:], tiles[0]), axis=1, keepdims=True)
        inverse = 1.0 / jnp.maximum(degree, 1.0)
        for b in range(2):
            weight_of[b, at_rows] = jnp.broadcast_to(coefficients[r, b] * inverse, (block, block))
        return carry

    lax.fori_loop(0, pairs, build, 0)
    loads[1].wait()
    cot_t[...] = jnp.swapaxes(cotangent[...], 0, 1)

    def mix(c):
        cols = slice(c * part, (c + 1) * part)
        pltpu.make_async_copy(arrived.at[c], arrived.at[c], a_recv.at[c]).wait()
        for t in range(blocks):
            lo, hi = t * relations * block, (t + 1) * relations * block
            aggregate = dot(adjacency[lo:hi, :rows], features[:, cols]) + dot(
                adjacency[lo:hi, rows:], arrived[c]
            )
            for b in range(2):
                for u in range(part // 128):
                    lanes = slice(u * 128, (u + 1) * 128)
                    value = weight_of[b, lo : lo + block] * aggregate[:block, lanes]
                    for r in range(1, relations):
                        value = value + (
                            weight_of[b, lo + r * block : lo + (r + 1) * block]
                            * aggregate[r * block : (r + 1) * block, lanes]
                        )
                    mixed[b, c, t * block : (t + 1) * block, lanes] = value.astype(BF16)
        core_out[c] = dot(cot_t[...], mixed[1 - core, c]).astype(BF16)
        pltpu.make_async_remote_copy(
            src_ref=core_out.at[c],
            dst_ref=core_in.at[c],
            send_sem=c_send.at[c],
            recv_sem=c_recv.at[c],
            device_id={"group": g + 1 - 2 * core, "outer": o},
            device_id_type=MESH,
        ).start()
        total[c] = dot(cot_t[...], mixed[core, c])

    def along(kind, i):
        if kind == 0:
            there = (z + i) % zs
            return there, there * xs + x
        there = (x + i) % xs
        return there, z * xs + there

    def spread_first(c):
        pltpu.make_async_copy(core_in.at[c], core_in.at[c], c_recv.at[c]).wait()
        whole = total[c] + core_in[c].astype(F32)
        by_z = whole[:, :half]
        by_x = whole[:, half:]
        by_x = jnp.concatenate(
            [
                by_x[zi * z_rows + xi * tail : zi * z_rows + (xi + 1) * tail]
                for xi in range(xs)
                for zi in range(zs)
            ],
            axis=0,
        )
        for kind, value in ((0, by_z), (1, by_x)):
            total[c, :, kind * half : (kind + 1) * half] = value
            first_out[c, kind] = value.astype(BF16)
        for kind, count in ((0, zs), (1, xs)):
            size = out_cols // count

            def send(i, carry, kind=kind, size=size):
                there, outer = along(kind, i)
                pltpu.make_async_remote_copy(
                    src_ref=first_out.at[c, kind, pl.ds(pl.multiple_of(there * size, size), size)],
                    dst_ref=first_in.at[c, kind, i - 1],
                    send_sem=f_send.at[c, kind],
                    recv_sem=f_recv.at[c, kind],
                    device_id={"group": g, "outer": outer},
                    device_id_type=MESH,
                ).start()
                return carry

            lax.fori_loop(1, count, send, 0)

    def spread_second(c):
        for kind, count, mine in ((0, zs, z), (1, xs, x)):
            size = out_cols // count
            landed = first_in.at[c, kind]
            pltpu.make_async_copy(landed, landed, f_recv.at[c, kind]).wait()
            held = total[
                c, pl.ds(pl.multiple_of(mine * size, size), size), kind * half : (kind + 1) * half
            ]
            for i in range(count - 1):
                held = held + first_in[c, kind, i].astype(F32)
            second_out[c, kind] = held
        for kind, count in ((0, xs), (1, zs)):

            def send(i, carry, kind=kind):
                there, outer = along(1 - kind, i)
                pltpu.make_async_remote_copy(
                    src_ref=second_out.at[c, kind, pl.ds(pl.multiple_of(there * tail, tail), tail)],
                    dst_ref=second_in.at[c, kind, i - 1],
                    send_sem=s_send.at[c, kind],
                    recv_sem=s_recv.at[c, kind],
                    device_id={"group": g, "outer": outer},
                    device_id_type=MESH,
                ).start()
                return carry

            lax.fori_loop(1, count, send, 0)

    def spread_third(c):
        for kind, count, mine in ((0, xs, x), (1, zs, z)):
            landed = second_in.at[c, kind]
            pltpu.make_async_copy(landed, landed, s_recv.at[c, kind]).wait()
            held = second_out[c, kind, pl.ds(pl.multiple_of(mine * tail, tail), tail)]
            for i in range(count - 1):
                held = held + second_in[c, kind, i]
            for u in range(half // 128):
                y = (c * part + kind * half) // 128 + u
                third_out[y] = held[:, u * 128 : (u + 1) * 128]
                for q in (2 * y, 2 * y + 1):

                    @pl.when(q != g)
                    def _(y=y, q=q):
                        pltpu.make_async_remote_copy(
                            src_ref=third_out.at[y],
                            dst_ref=third_in.at[g],
                            send_sem=t_send,
                            recv_sem=t_recv,
                            device_id={"group": q, "outer": o},
                            device_id_type=MESH,
                        ).start()

                    @pl.when(q == g)
                    def _(y=y):
                        pltpu.make_async_copy(third_out.at[y], third_in.at[g], t_recv).start()

    for step in range(chunks):
        mix(step)
        if step >= 1:
            spread_second(step - 1)
        spread_first(step)
        if step >= 2:
            spread_third(step - 2)

    loads[2].wait()
    loads[3].wait()
    value = dot(features[...], own_weight[...])
    for b in range(2):
        for c in range(chunks):
            value = value + dot(mixed[b, c], basis[b, c * part : (c + 1) * part])
    layer[...] = value.astype(BF16)
    store = pltpu.make_async_copy(layer, layer_hbm, load_sem.at[4])
    store.start()

    if chunks >= 2:
        spread_third(chunks - 2)
    spread_second(chunks - 1)
    spread_third(chunks - 1)

    pltpu.make_async_copy(third_in, third_in, t_recv).wait()
    scale = 1.0 / math.sqrt(rows * groups * zs * xs)
    for b in range(2):
        value = third_in[b]
        for y in range(1, groups // 2):
            value = value + third_in[2 * y + b]
        turned[b] = jnp.swapaxes(value * scale, 0, 1)
        wide = width // groups
        grad_out[b] = turned[b, pl.ds(pl.multiple_of(core * wide, wide), wide)]

    store.wait()
    for c in range(chunks):
        sent = outgoing.at[c, : outgoing.shape[1] - peer_rows]
        pltpu.make_async_copy(sent, sent, a_send.at[c]).wait()
        pltpu.make_async_copy(core_out.at[c], core_out.at[c], c_send.at[c]).wait()
        for kind in (0, 1):
            pltpu.make_async_copy(
                first_in.at[c, kind], first_in.at[c, kind], f_send.at[c, kind]
            ).wait()
            pltpu.make_async_copy(
                second_in.at[c, kind], second_in.at[c, kind], s_send.at[c, kind]
            ).wait()
    sent = third_in.at[: groups - 1]
    pltpu.make_async_copy(sent, sent, t_send).wait()


def shards(
    mesh_sizes,
    features,
    basis_weights,
    self_weight,
    coefficients,
    counts,
    tile_source,
    send_rows,
    edge_rows,
    cotangent,
):
    groups, zs, xs = mesh_sizes
    rows, width = features.shape
    out_cols = cotangent.shape[1]
    blocks, relations, slots, block, _ = counts.shape
    chunks = min(CHUNKS, width // 256)
    part = width // chunks
    half = part // 2
    peers = groups * send_rows.shape[1]
    arriving = peers + 2 * edge_rows.shape[1]
    pairs = blocks * relations
    sizes = (groups, zs, xs, chunks, relations, slots, block)
    z_rows = out_cols // zs
    tail = z_rows // xs
    vmem = pl.BlockSpec(memory_space=pltpu.VMEM)
    smem = pl.BlockSpec(memory_space=pltpu.SMEM)
    anywhere = pl.BlockSpec(memory_space=pl.ANY)
    dma = pltpu.SemaphoreType.DMA
    return pl.pallas_call(
        functools.partial(layer_kernel, sizes),
        out_shape=(
            jax.ShapeDtypeStruct((rows, out_cols), BF16),
            jax.ShapeDtypeStruct((2, width // groups, tail), F32),
        ),
        in_specs=[vmem, anywhere, anywhere, smem, anywhere, smem, vmem, vmem, anywhere],
        out_specs=(anywhere, vmem),
        scratch_shapes=[
            pltpu.VMEM(counts.shape, jnp.int32),
            pltpu.VMEM(basis_weights.shape, BF16),
            pltpu.VMEM(self_weight.shape, BF16),
            pltpu.VMEM((rows, out_cols), BF16),
            pltpu.VMEM((out_cols, rows), BF16),
            pltpu.VMEM((pairs * block, rows + arriving), BF16),
            pltpu.VMEM((2, pairs * block, block), F32),
            pltpu.VMEM((chunks, arriving, part), BF16),
            pltpu.VMEM((chunks, arriving, part), BF16),
            pltpu.VMEM((2, chunks, rows, part), BF16),
            pltpu.VMEM((rows, out_cols), BF16),
            pltpu.VMEM((chunks, out_cols, part), BF16),
            pltpu.VMEM((chunks, out_cols, part), BF16),
            pltpu.VMEM((chunks, out_cols, part), F32),
            pltpu.VMEM((chunks, 2, out_cols, half), BF16),
            pltpu.VMEM((chunks, 2, zs - 1, z_rows, half), BF16),
            pltpu.VMEM((chunks, 2, z_rows, half), F32),
            pltpu.VMEM((chunks, 2, zs - 1, tail, half), F32),
            pltpu.VMEM((groups // 2, tail, 128), F32),
            pltpu.VMEM((groups, tail, 128), F32),
            pltpu.VMEM((2, 128, tail), F32),
            dma((5,)),
            dma((chunks,)),
            dma((chunks,)),
            dma((chunks,)),
            dma((chunks,)),
            dma((chunks, 2)),
            dma((chunks, 2)),
            dma((chunks, 2)),
            dma((chunks, 2)),
            dma,
            dma,
        ],
        compiler_params=pltpu.CompilerParams(
            collective_id=0, has_side_effects=True, vmem_limit_bytes=56 * 1024 * 1024
        ),
        cost_estimate=pl.CostEstimate(
            flops=3 * 10**9, bytes_accessed=6 * 10**6, transcendentals=0
        ),
        name="graph_layer",
    )(
        features,
        basis_weights,
        self_weight,
        coefficients,
        counts,
        tile_source,
        send_rows,
        edge_rows,
        cotangent,
    )


def solution(mesh):
    groups, outers = mesh.shape["group"], mesh.shape["outer"]
    side = math.isqrt(outers)
    return jax.shard_map(
        functools.partial(shards, (groups, side, side)),
        mesh=mesh,
        in_specs=(
            P(("group", "outer"), None),
            P(),
            P(),
            P(),
            P(("group", "outer"), None, None, None, None),
            P(("group", "outer"), None, None),
            P(("group", "outer"), None),
            P(("group", "outer"), None),
            P(("group", "outer"), None),
        ),
        out_specs=(P(("group", "outer"), None), P(None, "group", "outer")),
        check_vma=False,
    )
```

time: 390 us -> 74 us (0.19)
  waiting for transfers between devices: 310 us -> 0 us
  Pallas kernels: 0 us -> 67.3 us
  starting transfers between devices: 28.2 us -> 0 us
  between operations: 14.3 us -> 0.64 us
  matrix products: 11.9 us -> 0 us
  local copies, waits for them, and re-layouts: 15 us -> 5.79 us
  other arithmetic: 8.79 us -> 0 us
    reduce_scatter x1 -> x0, waiting for transfers between devices: 245 us -> none  [shards(): lax.psum_scatter(grad_term, 'outer', scatter_dimension=2, tiled=True)]
    pallas_call x0 -> x1, Pallas kernels: none -> 67.3 us  [shards(): pl.pallas_call(functools.partial(layer_kernel, sizes), out_shape=(jax.Sha...]
    unnamed x3 -> x0, waiting for transfers between devices: 62 us -> none
    all_to_all x1 -> x0, starting transfers between devices: 15.4 us -> none  [shards(): lax.all_to_all(outgoing, 'group', split_axis=0, concat_axis=0, tiled=True)]
    ppermute x2 -> x0, starting transfers between devices: 12.7 us -> none  [the longest x1 10.8 us: with_halo(): lax.ppermute(lax.slice_in_dim(block, 0, width, axis=dim), axis, backward)]
    dot_general x5 -> x0, matrix products: 11.9 us -> none  [the longest x1 4.77 us: shards(): jnp.einsum('drkij,drkjh->drih', counts.astype(jnp.bfloat16), chosen, pref...]
    gather x3 -> x0, local copies, waits for them, and re-layouts: 8.25 us -> none  [the longest x1 4.36 us: shards(): jnp.take(stacked, tile_source.reshape(-1), axis=0)]
    another operation x1 -> x0, other arithmetic: 4.24 us -> none
  transfers between devices with their start and end apart: 5 -> 0, of which waited for: 4 -> 0; matrix products, arithmetic and copies ran while one was open for 2% -> 0% of each run, Pallas kernels for 0% -> 0%
where the time goes in v1:
time: 74 us; the launch traced here: 73.8 us
  Pallas kernels  67.3 us (91%)
  local copies, waits for them, and re-layouts  5.79 us (8%)
    pallas_call x1, Pallas kernels, shards(): pl.pallas_call(functools.partial(layer_kernel, sizes), out_shape=(jax.Sha...  67.3 us
    unnamed x3, local copies, waits for them, and re-layouts  4.28 us
    pallas_call x1, local copies, waits for them, and re-layouts, shards(): pl.pallas_call(functools.partial(layer_kernel, sizes), out_shape=(jax.Sha...  1.51 us

profile of v1, /device:TPU:113, one launch (start us, length us, event | category | flops | bytes accessed | tf_op | source)
XLA Modules:
  0.0 73.8 jit_solution(6480736357838539652)
XLA Ops:
  0.6 1.3 %copy.11.coefficients = f32[3,2]{1,0:T(4,128)} copy(f32[3,2]{0,1:T(2,128)} %param.12) | data formatting | bytes 48 | tf_op args[3]
  2.0 1.3 %copy.12.tile_source = s32[2,3,4]{2,1,0:T(4,128)} copy(s32[2,3,4]{2,0,1:T(2,128)} %param.14) | data formatting | bytes 192 | tf_op args[5]
  3.2 67.3 %graph_layer.1 = (bf16[256,512]{1,0:T(8,128)(2,1)}, f32[2,64,8]{2,1,0:T(8,128)}) custom-call(bf16[256,1024]{1,0:T(8,128)(2,1)} %features.1, bf16[2,1024,512]{2,1,0:T(8,128)(2,1)} %basis_hbm.1, bf16[1024,512]{1,0:T(8,128)(2,1)} %self_hbm.1, f32[3,2]{1,0:T(4,128)} %copy.11.coefficients, s32[2,3,4,128,128]{4,3,2,1,0:T(8,128)} %counts_hbm.1, ...), custom_call_target="tpu_custom_call" | custom-call | flops 3000000000 | bytes 6000000 | tf_op jit(solution)/shard_map/graph_layer/pallas_call | solution.py:402
  70.6 1.5 %copy.13 = f32[2,64,8]{1,2,0:T(8,128)} copy(f32[2,64,8]{2,1,0:T(8,128)} %get-tuple-element.3) | data formatting | bytes 8192 | tf_op jit(solution)/shard_map/graph_layer/pallas_call | solution.py:402
  72.1 1.7 %copy.15 = bf16[256,512]{1,0:T(8,128)(2,1)} copy(bf16[256,512]{1,0:T(8,128)(2,1)} %get-tuple-element.6) | data formatting | bytes 524288

commit v2 on v1

--- a/solution.py
+++ b/solution.py
@@ -10,6 +10,7 @@
 
 MESH = pl.DeviceIdType.MESH
 CHUNKS = 4
+AHEAD = 3
 F32 = jnp.float32
 BF16 = jnp.bfloat16
 
@@ -25,7 +26,7 @@
 
 def layer_kernel(
     sizes,
-    features,
+    features_hbm,
     basis_hbm,
     self_hbm,
     coefficients,
@@ -36,6 +37,7 @@
     cotangent_hbm,
     layer_hbm,
     grad_out,
+    features,
     counts,
     basis,
     own_weight,
@@ -56,7 +58,6 @@
     second_in,
     third_out,
     third_in,
-    turned,
     load_sem,
     a_send,
     a_recv,
@@ -118,8 +119,9 @@
         pltpu.make_async_copy(cotangent_hbm, cotangent, load_sem.at[1]),
         pltpu.make_async_copy(self_hbm, own_weight, load_sem.at[2]),
         pltpu.make_async_copy(basis_hbm, basis, load_sem.at[3]),
+        pltpu.make_async_copy(features_hbm, features, load_sem.at[5]),
     ]
-    for load in loads:
+    for load in loads[-1:] + loads[:-1]:
         load.start()
 
     slot_rows = jnp.broadcast_to(
@@ -140,15 +142,13 @@
         for side in (0, 1)
     ]
     pick = one_hot_of(jnp.concatenate([peer_index] + rim_index, axis=0), rows)
-    for c in range(chunks):
-        outgoing[c] = dot(pick, features[:, c * part : (c + 1) * part]).astype(BF16)
-
+    loads[-1].wait()
+    outgoing[0] = dot(pick, features[:, :part]).astype(BF16)
     pl.semaphore_wait(barrier, groups - 1 + xs - 1 + zs - 1 + 2)
 
     own = pl.ds(pl.multiple_of(g * peer_rows, peer_rows), peer_rows)
-    for c in range(chunks):
-
-        def send_peer(i, carry, c=c):
+    def exchange(c):
+        def send_peer(i, carry):
             q = (g + i) % groups
             theirs = pl.ds(pl.multiple_of(q * peer_rows, peer_rows), peer_rows)
             pltpu.make_async_remote_copy(
@@ -176,12 +176,19 @@
                 device_id_type=MESH,
             ).start()
 
+    for c in range(chunks):
+        if c >= 1:
+            outgoing[c] = dot(pick, features[:, c * part : (c + 1) * part]).astype(BF16)
+        if c < AHEAD:
+            exchange(c)
+
     loads[0].wait()
 
     def build(p, carry):
         t, r = p // relations, p % relations
         tiles = [counts[t, r, k].astype(F32) for k in range(slots)]
-        named = [tile_source[t, r, k] for k in range(slots)]
+        row = tile_source[r, pl.ds(t, 1)]
+        named = [jnp.broadcast_to(row[:, k : k + 1], (block, block)) for k in range(slots)]
         at_rows = pl.ds(pl.multiple_of(p * block, block), block)
         for s in range(sources):
             held = jnp.zeros((block, block), F32)
@@ -191,7 +198,11 @@
         degree = jnp.sum(sum(tiles[1:], tiles[0]), axis=1, keepdims=True)
         inverse = 1.0 / jnp.maximum(degree, 1.0)
         for b in range(2):
-            weight_of[b, at_rows] = jnp.broadcast_to(coefficients[r, b] * inverse, (block, block))
+            lanes = lax.broadcasted_iota(jnp.int32, (1, relations), 1)
+            gain = jnp.sum(
+                jnp.where(lanes == r, coefficients[b : b + 1], 0.0), axis=1, keepdims=True
+            )
+            weight_of[b, at_rows] = jnp.broadcast_to(gain * inverse, (block, block))
         return carry
 
     lax.fori_loop(0, pairs, build, 0)
@@ -201,6 +212,8 @@
     def mix(c):
         cols = slice(c * part, (c + 1) * part)
         pltpu.make_async_copy(arrived.at[c], arrived.at[c], a_recv.at[c]).wait()
+        if c + AHEAD < chunks:
+            exchange(c + AHEAD)
         for t in range(blocks):
             lo, hi = t * relations * block, (t + 1) * relations * block
             aggregate = dot(adjacency[lo:hi, :rows], features[:, cols]) + dot(
@@ -247,10 +260,9 @@
             ],
             axis=0,
         )
-        for kind, value in ((0, by_z), (1, by_x)):
+        for kind, count, value in ((0, zs, by_z), (1, xs, by_x)):
+            first_out[c, kind] = value.astype(BF16)
             total[c, :, kind * half : (kind + 1) * half] = value
-            first_out[c, kind] = value.astype(BF16)
-        for kind, count in ((0, zs), (1, xs)):
             size = out_cols // count
 
             def send(i, carry, kind=kind, size=size):
@@ -323,11 +335,11 @@
 
     for step in range(chunks):
         mix(step)
-        if step >= 1:
-            spread_second(step - 1)
         spread_first(step)
         if step >= 2:
-            spread_third(step - 2)
+            spread_second(step - 2)
+        if step >= 3:
+            spread_third(step - 3)
 
     loads[2].wait()
     loads[3].wait()
@@ -340,8 +352,12 @@
     store.start()
 
     if chunks >= 2:
+        spread_second(chunks - 2)
+    if chunks >= 3:
+        spread_third(chunks - 3)
+    spread_second(chunks - 1)
+    if chunks >= 2:
         spread_third(chunks - 2)
-    spread_second(chunks - 1)
     spread_third(chunks - 1)
 
     pltpu.make_async_copy(third_in, third_in, t_recv).wait()
@@ -350,9 +366,9 @@
         value = third_in[b]
         for y in range(1, groups // 2):
             value = value + third_in[2 * y + b]
-        turned[b] = jnp.swapaxes(value * scale, 0, 1)
+        value = value * scale
         wide = width // groups
-        grad_out[b] = turned[b, pl.ds(pl.multiple_of(core * wide, wide), wide)]
+        grad_out[b] = jnp.where(core == 0, value[:, :wide], value[:, wide:])
 
     store.wait()
     for c in range(chunks):
@@ -396,18 +412,18 @@
     z_rows = out_cols // zs
     tail = z_rows // xs
     vmem = pl.BlockSpec(memory_space=pltpu.VMEM)
-    smem = pl.BlockSpec(memory_space=pltpu.SMEM)
     anywhere = pl.BlockSpec(memory_space=pl.ANY)
     dma = pltpu.SemaphoreType.DMA
-    return pl.pallas_call(
+    layer_out, grad = pl.pallas_call(
         functools.partial(layer_kernel, sizes),
         out_shape=(
             jax.ShapeDtypeStruct((rows, out_cols), BF16),
-            jax.ShapeDtypeStruct((2, width // groups, tail), F32),
+            jax.ShapeDtypeStruct((2, tail, width // groups), F32),
         ),
-        in_specs=[vmem, anywhere, anywhere, smem, anywhere, smem, vmem, vmem, anywhere],
+        in_specs=[anywhere, anywhere, anywhere, vmem, anywhere, vmem, vmem, vmem, anywhere],
         out_specs=(anywhere, vmem),
         scratch_shapes=[
+            pltpu.VMEM(features.shape, BF16),
             pltpu.VMEM(counts.shape, jnp.int32),
             pltpu.VMEM(basis_weights.shape, BF16),
             pltpu.VMEM(self_weight.shape, BF16),
@@ -428,8 +444,7 @@
             pltpu.VMEM((chunks, 2, zs - 1, tail, half), F32),
             pltpu.VMEM((groups // 2, tail, 128), F32),
             pltpu.VMEM((groups, tail, 128), F32),
-            pltpu.VMEM((2, 128, tail), F32),
-            dma((5,)),
+            dma((6,)),
             dma((chunks,)),
             dma((chunks,)),
             dma((chunks,)),
@@ -452,13 +467,14 @@
         features,
         basis_weights,
         self_weight,
-        coefficients,
+        coefficients.T,
         counts,
-        tile_source,
+        tile_source.transpose(1, 0, 2),
         send_rows,
         edge_rows,
         cotangent,
     )
+    return layer_out, grad.transpose(0, 2, 1)
 
 
 def solution(mesh):

time: 74 us -> 60.5 us (0.82)
  Pallas kernels: 67.3 us -> 56.6 us
  local copies, waits for them, and re-layouts: 5.79 us -> 2.96 us
    pallas_call x1, Pallas kernels: 67.3 us -> 56.6 us  [shards(): pl.pallas_call(functools.partial(layer_kernel, sizes), out_shape=(jax.Sha...]
    pallas_call x1 -> x0, local copies, waits for them, and re-layouts: 1.51 us -> none  [shards(): pl.pallas_call(functools.partial(layer_kernel, sizes), out_shape=(jax.Sha...]
    unnamed x3 -> x2, local copies, waits for them, and re-layouts: 4.28 us -> 2.96 us
where the time goes in v2:
time: 60.5 us; the launch traced here: 60.2 us
  Pallas kernels  56.6 us (94%)
  local copies, waits for them, and re-layouts  2.96 us (5%)
  between operations  0.64 us (1%)
    pallas_call x1, Pallas kernels, shards(): pl.pallas_call(functools.partial(layer_kernel, sizes), out_shape=(jax.Sha...  56.6 us
    unnamed x2, local copies, waits for them, and re-layouts  2.96 us

profile of v2, /device:TPU:113, one launch (start us, length us, event | category | flops | bytes accessed | tf_op | source)
XLA Modules:
  0.0 60.2 jit_solution(17410524510887486804)
XLA Ops:
  0.6 56.6 %graph_layer.1 = (bf16[256,512]{1,0:T(8,128)(2,1)}, f32[2,8,64]{2,1,0:T(8,128)}) custom-call(bf16[256,1024]{1,0:T(8,128)(2,1)} %features_hbm.1, bf16[2,1024,512]{2,1,0:T(8,128)(2,1)} %basis_hbm.1, bf16[1024,512]{1,0:T(8,128)(2,1)} %self_hbm.1, f32[2,3]{1,0:T(2,128)} %bitcast.5, s32[2,3,4,128,128]{4,3,2,1,0:T(8,128)} %counts_hbm.1, s32[3,2,4]{2,1,0:T(2,128)} %bitcast.4, ...), custom_call_target="tpu_custom_call" | custom-call | flops 3000000000 | bytes 6000000 | tf_op jit(solution)/shard_map/graph_layer/pallas_call | solution.py:417
  57.2 1.7 %copy.13 = bf16[256,512]{1,0:T(8,128)(2,1)} copy(bf16[256,512]{1,0:T(8,128)(2,1)} %get-tuple-element.8) | data formatting | bytes 524288
  58.9 1.3 %copy.14 = f32[2,64,8]{1,2,0:T(8,128)} copy(f32[2,64,8]{1,2,0:T(8,128)} %bitcast.3) | data formatting | bytes 8192

commit v3 on v2

--- a/solution.py
+++ b/solution.py
@@ -29,15 +29,19 @@
     features_hbm,
     basis_hbm,
     self_hbm,
-    coefficients,
+    coefficients_hbm,
     counts_hbm,
-    tile_source,
-    send_rows,
-    edge_rows,
+    tile_source_hbm,
+    send_rows_hbm,
+    edge_rows_hbm,
     cotangent_hbm,
     layer_hbm,
     grad_out,
     features,
+    coefficients,
+    tile_source,
+    send_rows,
+    edge_rows,
     counts,
     basis,
     own_weight,
@@ -73,8 +77,8 @@
     groups, zs, xs, chunks, relations, slots, block = sizes
     g = lax.axis_index("group")
     o = lax.axis_index("outer")
-    z, x = o // xs, o % xs
-    core = g % 2
+    z, x = lax.div(o, xs), lax.rem(o, xs)
+    core = lax.rem(g, 2)
     rows, width = features.shape
     out_cols = cotangent.shape[1]
     peer_rows = send_rows.shape[1]
@@ -87,6 +91,21 @@
     z_rows = out_cols // zs
     tail = z_rows // xs
 
+    def load(source, target, i):
+        copy = pltpu.make_async_copy(source, target, load_sem.at[i])
+        copy.start()
+        return copy
+
+    send_load = load(send_rows_hbm, send_rows, 6)
+    edge_load = load(edge_rows_hbm, edge_rows, 7)
+    feature_load = load(features_hbm, features, 5)
+    gain_load = load(coefficients_hbm, coefficients, 8)
+    source_load = load(tile_source_hbm, tile_source, 9)
+    counts_load = load(counts_hbm, counts, 0)
+    cotangent_load = load(cotangent_hbm, cotangent, 1)
+    own_load = load(self_hbm, own_weight, 2)
+    basis_load = load(basis_hbm, basis, 3)
+
     barrier = pltpu.get_barrier_semaphore()
 
     def greet(group, outer):
@@ -95,35 +114,27 @@
         )
 
     def greet_group(i, carry):
-        greet((g + i) % groups, o)
+        greet(lax.rem(g + i, groups), o)
         return carry
 
     def greet_x(i, carry):
-        greet(g, z * xs + (x + i) % xs)
+        greet(g, z * xs + lax.rem(x + i, xs))
         return carry
 
     def greet_z(i, carry):
-        greet(g, ((z + i) % zs) * xs + x)
+        greet(g, lax.rem(z + i, zs) * xs + x)
         return carry
 
-    upper = (o + 1) % (zs * xs)
-    lower = (o + zs * xs - 1) % (zs * xs)
+    upper = lax.rem(o + 1, zs * xs)
+    lower = lax.rem(o + zs * xs - 1, zs * xs)
     lax.fori_loop(1, groups, greet_group, 0)
     lax.fori_loop(1, xs, greet_x, 0)
     lax.fori_loop(1, zs, greet_z, 0)
     greet(g, upper)
     greet(g, lower)
 
-    loads = [
-        pltpu.make_async_copy(counts_hbm, counts, load_sem.at[0]),
-        pltpu.make_async_copy(cotangent_hbm, cotangent, load_sem.at[1]),
-        pltpu.make_async_copy(self_hbm, own_weight, load_sem.at[2]),
-        pltpu.make_async_copy(basis_hbm, basis, load_sem.at[3]),
-        pltpu.make_async_copy(features_hbm, features, load_sem.at[5]),
-    ]
-    for load in loads[-1:] + loads[:-1]:
-        load.start()
-
+    send_load.wait()
+    edge_load.wait()
     slot_rows = jnp.broadcast_to(
         send_rows[...][:, None, :], (groups, peer_rows, peer_rows)
     ).reshape(incoming, peer_rows)
@@ -142,14 +153,14 @@
         for side in (0, 1)
     ]
     pick = one_hot_of(jnp.concatenate([peer_index] + rim_index, axis=0), rows)
-    loads[-1].wait()
+    feature_load.wait()
     outgoing[0] = dot(pick, features[:, :part]).astype(BF16)
     pl.semaphore_wait(barrier, groups - 1 + xs - 1 + zs - 1 + 2)
 
     own = pl.ds(pl.multiple_of(g * peer_rows, peer_rows), peer_rows)
     def exchange(c):
         def send_peer(i, carry):
-            q = (g + i) % groups
+            q = lax.rem(g + i, groups)
             theirs = pl.ds(pl.multiple_of(q * peer_rows, peer_rows), peer_rows)
             pltpu.make_async_remote_copy(
                 src_ref=outgoing.at[c, theirs],
@@ -182,10 +193,12 @@
         if c < AHEAD:
             exchange(c)
 
-    loads[0].wait()
+    gain_load.wait()
+    source_load.wait()
+    counts_load.wait()
 
     def build(p, carry):
-        t, r = p // relations, p % relations
+        t, r = lax.div(p, relations), lax.rem(p, relations)
         tiles = [counts[t, r, k].astype(F32) for k in range(slots)]
         row = tile_source[r, pl.ds(t, 1)]
         named = [jnp.broadcast_to(row[:, k : k + 1], (block, block)) for k in range(slots)]
@@ -206,7 +219,7 @@
         return carry
 
     lax.fori_loop(0, pairs, build, 0)
-    loads[1].wait()
+    cotangent_load.wait()
     cot_t[...] = jnp.swapaxes(cotangent[...], 0, 1)
 
     def mix(c):
@@ -242,9 +255,9 @@
 
     def along(kind, i):
         if kind == 0:
-            there = (z + i) % zs
+            there = lax.rem(z + i, zs)
             return there, there * xs + x
-        there = (x + i) % xs
+        there = lax.rem(x + i, xs)
         return there, z * xs + there
 
     def spread_first(c):
@@ -290,7 +303,6 @@
             for i in range(count - 1):
                 held = held + first_in[c, kind, i].astype(F32)
             second_out[c, kind] = held
-        for kind, count in ((0, xs), (1, zs)):
 
             def send(i, carry, kind=kind):
                 there, outer = along(1 - kind, i)
@@ -304,7 +316,7 @@
                 ).start()
                 return carry
 
-            lax.fori_loop(1, count, send, 0)
+            lax.fori_loop(1, (xs, zs)[kind], send, 0)
 
     def spread_third(c):
         for kind, count, mine in ((0, xs, x), (1, zs, z)):
@@ -341,8 +353,8 @@
         if step >= 3:
             spread_third(step - 3)
 
-    loads[2].wait()
-    loads[3].wait()
+    own_load.wait()
+    basis_load.wait()
     value = dot(features[...], own_weight[...])
     for b in range(2):
         for c in range(chunks):
@@ -384,6 +396,24 @@
             ).wait()
     sent = third_in.at[: groups - 1]
     pltpu.make_async_copy(sent, sent, t_send).wait()
+
+
+def hand_over(layer, grad, layer_out, grad_out, layer_held, grad_held, sem):
+    arriving = [
+        pltpu.make_async_copy(layer, layer_held, sem.at[0]),
+        pltpu.make_async_copy(grad, grad_held, sem.at[1]),
+    ]
+    leaving = [
+        pltpu.make_async_copy(layer_held, layer_out, sem.at[2]),
+        pltpu.make_async_copy(grad_held, grad_out, sem.at[3]),
+    ]
+    for copy in arriving:
+        copy.start()
+    for copy, then in zip(arriving, leaving):
+        copy.wait()
+        then.start()
+    for copy in leaving:
+        copy.wait()
 
 
 def shards(
@@ -420,10 +450,14 @@
             jax.ShapeDtypeStruct((rows, out_cols), BF16),
             jax.ShapeDtypeStruct((2, tail, width // groups), F32),
         ),
-        in_specs=[anywhere, anywhere, anywhere, vmem, anywhere, vmem, vmem, vmem, anywhere],
+        in_specs=[anywhere] * 9,
         out_specs=(anywhere, vmem),
         scratch_shapes=[
             pltpu.VMEM(features.shape, BF16),
+            pltpu.VMEM(coefficients.shape[::-1], F32),
+            pltpu.VMEM((relations, blocks, slots), jnp.int32),
+            pltpu.VMEM(send_rows.shape, jnp.int32),
+            pltpu.VMEM(edge_rows.shape, jnp.int32),
             pltpu.VMEM(counts.shape, jnp.int32),
             pltpu.VMEM(basis_weights.shape, BF16),
             pltpu.VMEM(self_weight.shape, BF16),
@@ -444,7 +478,7 @@
             pltpu.VMEM((chunks, 2, zs - 1, tail, half), F32),
             pltpu.VMEM((groups // 2, tail, 128), F32),
             pltpu.VMEM((groups, tail, 128), F32),
-            dma((6,)),
+            dma((10,)),
             dma((chunks,)),
             dma((chunks,)),
             dma((chunks,)),
@@ -474,6 +508,22 @@
         edge_rows,
         cotangent,
     )
+    layer_out, grad = pl.pallas_call(
+        hand_over,
+        out_shape=(
+            jax.ShapeDtypeStruct(layer_out.shape, layer_out.dtype),
+            jax.ShapeDtypeStruct(grad.shape, grad.dtype),
+        ),
+        in_specs=[anywhere, anywhere],
+        out_specs=(anywhere, anywhere),
+        scratch_shapes=[
+            pltpu.VMEM(layer_out.shape, layer_out.dtype),
+            pltpu.VMEM(grad.shape, grad.dtype),
+            dma((4,)),
+        ],
+        compiler_params=pltpu.CompilerParams(vmem_limit_bytes=56 * 1024 * 1024),
+        name="hand_over",
+    )(layer_out, grad)
     return layer_out, grad.transpose(0, 2, 1)
 
 

time: 60.5 us -> 58.6 us (0.969)
  local copies, waits for them, and re-layouts: 2.96 us -> 0 us
  Pallas kernels: 56.6 us -> 57.8 us
    unnamed x2 -> x0, local copies, waits for them, and re-layouts: 2.96 us -> none
    pallas_call x0 -> x1, Pallas kernels: none -> 1.69 us  [shards(): pl.pallas_call(hand_over, out_shape=(jax.ShapeDtypeStruct(layer_out.shape...]
where the time goes in v3:
time: 58.6 us; the launch traced here: 58.4 us
  Pallas kernels  57.8 us (99%)
  between operations  0.64 us (1%)
    pallas_call x1, Pallas kernels, shards(): pl.pallas_call(functools.partial(layer_kernel, sizes), out_shape=(jax.Sha...  56.1 us
    pallas_call x1, Pallas kernels, shards(): pl.pallas_call(hand_over, out_shape=(jax.ShapeDtypeStruct(layer_out.shape...  1.69 us

profile of v3, /device:TPU:113, one launch (start us, length us, event | category | flops | bytes accessed | tf_op | source)
XLA Modules:
  0.0 58.4 jit_solution(18003683249000967541)
XLA Ops:
  0.6 56.1 %graph_layer.1 = (bf16[256,512]{1,0:T(8,128)(2,1)}, f32[2,8,64]{2,1,0:T(8,128)}) custom-call(bf16[256,1024]{1,0:T(8,128)(2,1)} %features_hbm.1, bf16[2,1024,512]{2,1,0:T(8,128)(2,1)} %basis_hbm.1, bf16[1024,512]{1,0:T(8,128)(2,1)} %self_hbm.1, f32[2,3]{1,0:T(2,128)} %bitcast.5, s32[2,3,4,128,128]{4,3,2,1,0:T(8,128)} %counts_hbm.1, s32[3,2,4]{2,1,0:T(2,128)} %bitcast.4, ...), custom_call_target="tpu_custom_call" | custom-call | flops 3000000000 | bytes 6000000 | tf_op jit(solution)/shard_map/graph_layer/pallas_call | solution.py:447
  56.7 1.7 %hand_over.1 = (bf16[256,512]{1,0:T(8,128)(2,1)}, f32[2,8,64]{2,1,0:T(8,128)}) custom-call(bf16[256,512]{1,0:T(8,128)(2,1)} %get-tuple-element.6.layer, f32[2,8,64]{2,1,0:T(8,128)} %get-tuple-element.7.grad), custom_call_target="tpu_custom_call" | custom-call | tf_op jit(solution)/shard_map/hand_over/pallas_call | solution.py:511

commit v4 on v3

--- a/solution.py
+++ b/solution.py
@@ -35,7 +35,7 @@
     send_rows_hbm,
     edge_rows_hbm,
     cotangent_hbm,
-    layer_hbm,
+    layer,
     grad_out,
     features,
     coefficients,
@@ -52,7 +52,6 @@
     outgoing,
     arrived,
     mixed,
-    layer,
     core_out,
     core_in,
     total,
@@ -101,10 +100,6 @@
     feature_load = load(features_hbm, features, 5)
     gain_load = load(coefficients_hbm, coefficients, 8)
     source_load = load(tile_source_hbm, tile_source, 9)
-    counts_load = load(counts_hbm, counts, 0)
-    cotangent_load = load(cotangent_hbm, cotangent, 1)
-    own_load = load(self_hbm, own_weight, 2)
-    basis_load = load(basis_hbm, basis, 3)
 
     barrier = pltpu.get_barrier_semaphore()
 
@@ -154,6 +149,8 @@
     ]
     pick = one_hot_of(jnp.concatenate([peer_index] + rim_index, axis=0), rows)
     feature_load.wait()
+    counts_load = load(counts_hbm, counts, 0)
+    cotangent_load = load(cotangent_hbm, cotangent, 1)
     outgoing[0] = dot(pick, features[:, :part]).astype(BF16)
     pl.semaphore_wait(barrier, groups - 1 + xs - 1 + zs - 1 + 2)
 
@@ -192,6 +189,9 @@
             outgoing[c] = dot(pick, features[:, c * part : (c + 1) * part]).astype(BF16)
         if c < AHEAD:
             exchange(c)
+
+    own_load = load(self_hbm, own_weight, 2)
+    basis_load = load(basis_hbm, basis, 3)
 
     gain_load.wait()
     source_load.wait()
@@ -360,8 +360,6 @@
         for c in range(chunks):
             value = value + dot(mixed[b, c], basis[b, c * part : (c + 1) * part])
     layer[...] = value.astype(BF16)
-    store = pltpu.make_async_copy(layer, layer_hbm, load_sem.at[4])
-    store.start()
 
     if chunks >= 2:
         spread_second(chunks - 2)
@@ -382,7 +380,6 @@
         wide = width // groups
         grad_out[b] = jnp.where(core == 0, value[:, :wide], value[:, wide:])
 
-    store.wait()
     for c in range(chunks):
         sent = outgoing.at[c, : outgoing.shape[1] - peer_rows]
         pltpu.make_async_copy(sent, sent, a_send.at[c]).wait()
@@ -398,21 +395,14 @@
     pltpu.make_async_copy(sent, sent, t_send).wait()
 
 
-def hand_over(layer, grad, layer_out, grad_out, layer_held, grad_held, sem):
-    arriving = [
-        pltpu.make_async_copy(layer, layer_held, sem.at[0]),
-        pltpu.make_async_copy(grad, grad_held, sem.at[1]),
+def hand_over(layer, grad, layer_out, grad_out, sem):
+    copies = [
+        pltpu.make_async_copy(layer, layer_out, sem.at[0]),
+        pltpu.make_async_copy(grad, grad_out, sem.at[1]),
     ]
-    leaving = [
-        pltpu.make_async_copy(layer_held, layer_out, sem.at[2]),
-        pltpu.make_async_copy(grad_held, grad_out, sem.at[3]),
-    ]
-    for copy in arriving:
+    for copy in copies:
         copy.start()
-    for copy, then in zip(arriving, leaving):
-        copy.wait()
-        then.start()
-    for copy in leaving:
+    for copy in copies:
         copy.wait()
 
 
@@ -447,11 +437,11 @@
     layer_out, grad = pl.pallas_call(
         functools.partial(layer_kernel, sizes),
         out_shape=(
-            jax.ShapeDtypeStruct((rows, out_cols), BF16),
-            jax.ShapeDtypeStruct((2, tail, width // groups), F32),
+            pltpu.VMEM((rows, out_cols), BF16),
+            pltpu.VMEM((2, tail, width // groups), F32),
         ),
         in_specs=[anywhere] * 9,
-        out_specs=(anywhere, vmem),
+        out_specs=(vmem, vmem),
         scratch_shapes=[
             pltpu.VMEM(features.shape, BF16),
             pltpu.VMEM(coefficients.shape[::-1], F32),
@@ -468,7 +458,6 @@
             pltpu.VMEM((chunks, arriving, part), BF16),
             pltpu.VMEM((chunks, arriving, part), BF16),
             pltpu.VMEM((2, chunks, rows, part), BF16),
-            pltpu.VMEM((rows, out_cols), BF16),
             pltpu.VMEM((chunks, out_cols, part), BF16),
             pltpu.VMEM((chunks, out_cols, part), BF16),
             pltpu.VMEM((chunks, out_cols, part), F32),
@@ -514,14 +503,10 @@
             jax.ShapeDtypeStruct(layer_out.shape, layer_out.dtype),
             jax.ShapeDtypeStruct(grad.shape, grad.dtype),
         ),
-        in_specs=[anywhere, anywhere],
+        in_specs=[vmem, vmem],
         out_specs=(anywhere, anywhere),
-        scratch_shapes=[
-            pltpu.VMEM(layer_out.shape, layer_out.dtype),
-            pltpu.VMEM(grad.shape, grad.dtype),
-            dma((4,)),
-        ],
-        compiler_params=pltpu.CompilerParams(vmem_limit_bytes=56 * 1024 * 1024),
+        scratch_shapes=[dma((2,))],
+        compiler_params=pltpu.CompilerParams(vmem_limit_bytes=4 * 1024 * 1024),
         name="hand_over",
     )(layer_out, grad)
     return layer_out, grad.transpose(0, 2, 1)

time: 58.6 us -> 57.1 us (0.974)
  Pallas kernels: 57.8 us -> 56.2 us
    pallas_call x1, Pallas kernels: 1.69 us -> 0.72 us  [shards(): pl.pallas_call(hand_over, out_shape=(jax.ShapeDtypeStruct(layer_out.shape...]
where the time goes in v4:
time: 57.1 us; the launch traced here: 56.9 us
  Pallas kernels  56.2 us (98%)
  between operations  0.64 us (1%)
    pallas_call x1, Pallas kernels, shards(): pl.pallas_call(functools.partial(layer_kernel, sizes), out_shape=(pltpu.V...  55.5 us

profile of v4, /device:TPU:113, one launch (start us, length us, event | category | flops | bytes accessed | tf_op | source)
XLA Modules:
  0.0 56.9 jit_solution(17822984989055188395)
XLA Ops:
  0.6 55.5 %graph_layer.1 = (bf16[256,512]{1,0:T(8,128)(2,1)S(1)}, f32[2,8,64]{2,1,0:T(8,128)S(1)}) custom-call(bf16[256,1024]{1,0:T(8,128)(2,1)} %features_hbm.1, bf16[2,1024,512]{2,1,0:T(8,128)(2,1)} %basis_hbm.1, bf16[1024,512]{1,0:T(8,128)(2,1)} %self_hbm.1, f32[2,3]{1,0:T(2,128)} %bitcast.5, s32[2,3,4,128,128]{4,3,2,1,0:T(8,128)} %counts_hbm.1, ...), custom_call_target="tpu_custom_call" | custom-call | flops 3000000000 | bytes 6000000 | tf_op jit(solution)/shard_map/graph_layer/pallas_call | solution.py:437
  56.2 0.7 %hand_over.1 = (bf16[256,512]{1,0:T(8,128)(2,1)}, f32[2,8,64]{2,1,0:T(8,128)}) custom-call(bf16[256,512]{1,0:T(8,128)(2,1)S(1)} %get-tuple-element.6.layer, f32[2,8,64]{2,1,0:T(8,128)S(1)} %get-tuple-element.7.grad), custom_call_target="tpu_custom_call" | custom-call | tf_op jit(solution)/shard_map/hand_over/pallas_call | solution.py:500

commit v5 on v4

--- a/solution.py
+++ b/solution.py
@@ -278,7 +278,8 @@
             total[c, :, kind * half : (kind + 1) * half] = value
             size = out_cols // count
 
-            def send(i, carry, kind=kind, size=size):
+            def send(i, carry, kind=kind, size=size, count=count):
+                i = lax.rem(3 * i, count)
                 there, outer = along(kind, i)
                 pltpu.make_async_remote_copy(
                     src_ref=first_out.at[c, kind, pl.ds(pl.multiple_of(there * size, size), size)],
@@ -305,6 +306,7 @@
             second_out[c, kind] = held
 
             def send(i, carry, kind=kind):
+                i = lax.rem(3 * i, (xs, zs)[kind])
                 there, outer = along(1 - kind, i)
                 pltpu.make_async_remote_copy(
                     src_ref=second_out.at[c, kind, pl.ds(pl.multiple_of(there * tail, tail), tail)],

time: 57.1 us -> 57.1 us (level)
  no operation moved by 1% of the time
where the time goes in v5:
time: 57.1 us; the launch traced here: 56.9 us
  Pallas kernels  56.3 us (99%)
  between operations  0.64 us (1%)
    pallas_call x1, Pallas kernels, shards(): pl.pallas_call(functools.partial(layer_kernel, sizes), out_shape=(pltpu.V...  55.6 us

profile of v5, /device:TPU:113, one launch (start us, length us, event | category | flops | bytes accessed | tf_op | source)
XLA Modules:
  0.0 56.9 jit_solution(12996584361028869341)
XLA Ops:
  0.6 55.6 %graph_layer.1 = (bf16[256,512]{1,0:T(8,128)(2,1)S(1)}, f32[2,8,64]{2,1,0:T(8,128)S(1)}) custom-call(bf16[256,1024]{1,0:T(8,128)(2,1)} %features_hbm.1, bf16[2,1024,512]{2,1,0:T(8,128)(2,1)} %basis_hbm.1, bf16[1024,512]{1,0:T(8,128)(2,1)} %self_hbm.1, f32[2,3]{1,0:T(2,128)} %bitcast.5, s32[2,3,4,128,128]{4,3,2,1,0:T(8,128)} %counts_hbm.1, ...), custom_call_target="tpu_custom_call" | custom-call | flops 3000000000 | bytes 6000000 | tf_op jit(solution)/shard_map/graph_layer/pallas_call | solution.py:439
  56.2 0.7 %hand_over.1 = (bf16[256,512]{1,0:T(8,128)(2,1)}, f32[2,8,64]{2,1,0:T(8,128)}) custom-call(bf16[256,512]{1,0:T(8,128)(2,1)S(1)} %get-tuple-element.6.layer, f32[2,8,64]{2,1,0:T(8,128)S(1)} %get-tuple-element.7.grad), custom_call_target="tpu_custom_call" | custom-call | tf_op jit(solution)/shard_map/hand_over/pallas_call | solution.py:502
